TPU v7x, 512 devices: a whole 4x4x16 slice. The times are simulated.
512 devices in a mesh: seq: 32 (over x, z_lo, core), head: 16 (over y, z_hi).
Axes of the slice: x: 4, y: 4, z: 16 (z_hi: 4, z_lo: 4; z = z_hi * 4 + z_lo), core: 2. Of those that a mesh axis runs over, the one named last changes fastest.
Arguments:
- out_grad: bfloat16 [8192, 4096], P('seq', 'head'), may hold values from -7.2 to 7.2
- x_in: bfloat16 [8192, 4096], P('seq', 'head'), may hold values from -6 to 6
- b_in: bfloat16 [8192, 128], P('seq'), may hold values from -2.5 to 2.5
- c_in: bfloat16 [8192, 128], P('seq'), may hold values from -2.5 to 2.5
- dt_raw: float32 [64, 8192], P('head', 'seq'), may hold values from -5.1 to -0.7
- dt_bias: float32 [64], P('head'), may hold values from -0.5 to 0.5
- a_log: float32 [64], P('head'), may hold values from -7.5 to 2.2
- d_skip: float32 [64], P('head'), may hold values from 0.5 to 1.5
- states: bfloat16 [32, 4096, 128], P('seq', 'head'), may hold values from -6 to 6
- w_out: bfloat16 [4096, 4096], P('head'), may hold values from -0.09375 to 0.09375
- w_in: bfloat16 [4096, 4096], P(None, 'head'), may hold values from -0.125 to 0.125
Outputs:
- in_grad: bfloat16 [4096, 8192], P('head', 'seq')
- bc_grad: bfloat16 [256, 8192], P('head', 'seq')
- dt_grad: float32 [64, 8192], P('head', 'seq')
- param_grad: float32 [3, 64], P(None, 'head')
All inputs are finite; a program needn't handle non-finite values.
Results may differ from a plain program's by a relative error of at most 0.015.
Values may be sent and summed in bfloat16 or wider, within the bound.
No kernel may reach another device: no remote copies, remote signals or barrier semaphores. Data moves between devices by JAX's collectives and lax.ppermute only.
A program may use at most 64 MiB of HBM per device.

v0:
```python
import jax
import jax.numpy as jnp
from jax import lax
from jax.sharding import PartitionSpec as P


def passed_along(value, axis, steps):
    count = lax.axis_size(axis)
    initial, last = (max(0, -steps), min(count, count - steps))
    return lax.ppermute(value, axis, [(source, source + steps) for source in range(initial, last)])


def shards(out_grad, x_in, b_in, c_in, dt_raw, dt_bias, a_log, d_skip, states, w_out, w_in):
    tokens_here, inner_here = x_in.shape
    group_heads = dt_raw.shape[0]
    head_dim = inner_here // group_heads
    state_dim = b_in.shape[1]
    contract_last = (((1,), (1,)), ((), ()))
    head_sum = lax.dot_general(
        lax.all_gather(out_grad, "head", axis=1, tiled=True),
        w_out,
        contract_last,
        preferred_element_type=jnp.float32,
    )
    dy_heads = head_sum.astype(jnp.bfloat16).reshape(tokens_here, group_heads, head_dim)
    dy_wide = dy_heads.astype(jnp.float32)
    x_heads = x_in.reshape(tokens_here, group_heads, head_dim)
    x_wide = x_heads.astype(jnp.float32)
    decay_rate = jnp.exp(a_log)
    step_size = jax.nn.softplus(dt_raw + dt_bias[:, None])
    log_step = -decay_rate[:, None] * step_size
    cumlog = jnp.cumsum(log_step, axis=1)
    positions = jnp.arange(tokens_here)
    causal = positions[:, None] >= positions[None, :]
    log_gaps = cumlog[:, :, None] - cumlog[:, None, :]
    decay_mask = jnp.where(causal[None], jnp.exp(jnp.minimum(log_gaps, 0.0)), 0.0)
    scores = lax.dot_general(c_in, b_in, contract_last, preferred_element_type=jnp.float32)
    step_rows = step_size.T
    x_scaled = (x_wide * step_rows[:, :, None]).astype(jnp.bfloat16)
    pair_dots = jnp.einsum("ihp,jhp->hij", dy_heads, x_scaled, preferred_element_type=jnp.float32)
    kernel = (scores[None] * decay_mask).astype(jnp.bfloat16)
    intra_back = jnp.einsum("hij,ihp->jhp", kernel, dy_heads, preferred_element_type=jnp.float32)
    masked_dots = (pair_dots * decay_mask).astype(jnp.bfloat16)
    start_decay = jnp.exp(cumlog)
    dy_decay = (dy_wide * start_decay.T[:, :, None]).astype(jnp.bfloat16)
    local_state = jnp.einsum("ihp,in->hpn", dy_decay, c_in, preferred_element_type=jnp.float32)
    end_total = jnp.exp(cumlog[:, -1])
    entry_state = states.reshape(group_heads, head_dim, state_dim)
    db_intra = jnp.einsum("hij,in->nj", masked_dots, c_in, preferred_element_type=jnp.float32)
    dc_intra = jnp.einsum("hij,jn->ni", masked_dots, b_in, preferred_element_type=jnp.float32)
    dc_entry = jnp.einsum("ihp,hpn->ni", dy_decay, entry_state, preferred_element_type=jnp.float32)
    ystate = jnp.einsum("in,hpn->ihp", c_in, entry_state, preferred_element_type=jnp.float32)
    pair_weight = pair_dots * scores[None] * decay_mask
    state_terms = start_decay * jnp.sum(dy_wide * ystate, axis=2).T
    skip_terms = jnp.sum(dy_wide * x_wide, axis=(0, 2))

    def relay_turn(turn_index, held_state):
        return passed_along(end_total[:, None, None] * held_state + local_state, "seq", -1)

    carried = lax.fori_loop(0, lax.axis_size("seq") - 1, relay_turn, jnp.zeros_like(local_state))
    carried_bf = carried.astype(jnp.bfloat16)
    state_back = jnp.einsum("jn,hpn->jhp", b_in, carried_bf, preferred_element_type=jnp.float32)
    end_decay = jnp.exp(cumlog[:, -1:] - cumlog)
    end_weight = (step_size * end_decay).T
    x_grad = (
        (
            step_rows[:, :, None] * intra_back
            + end_weight[:, :, None] * state_back
            + d_skip[None, :, None] * dy_wide
        )
        .astype(jnp.bfloat16)
        .reshape(tokens_here, inner_here)
    )
    x_end = (x_wide * end_weight[:, :, None]).astype(jnp.bfloat16)
    db_entry = jnp.einsum("jhp,hpn->nj", x_end, carried_bf, preferred_element_type=jnp.float32)
    bc_part = jnp.concatenate([db_intra + db_entry, dc_intra + dc_entry], axis=0)
    end_terms = end_weight.T * jnp.sum(x_wide * state_back, axis=2).T
    cum_grad = pair_weight.sum(axis=2) - pair_weight.sum(axis=1) + state_terms - end_terms
    tail_grad = end_terms.sum(axis=1) + end_total * jnp.sum(
        entry_state.astype(jnp.float32) * carried, axis=(1, 2)
    )
    cum_grad = cum_grad.at[:, -1].add(tail_grad)
    step_grad = jnp.cumsum(cum_grad[:, ::-1], axis=1)[:, ::-1]
    dt_sum = (
        -decay_rate[:, None] * step_grad
        + jnp.sum(x_wide * (intra_back + end_decay.T[:, :, None] * state_back), axis=2).T
    )
    dt_grad = dt_sum * jax.nn.sigmoid(dt_raw + dt_bias[:, None])
    param_terms = jnp.stack(
        [jnp.sum(step_grad * log_step, axis=1), skip_terms, jnp.sum(dt_grad, axis=1)]
    )
    in_part = lax.psum_scatter(
        lax.dot_general(w_in, x_grad, contract_last, preferred_element_type=jnp.float32).astype(
            jnp.bfloat16
        ),
        "head",
        scatter_dimension=0,
        tiled=True,
    )
    bc_sum = lax.psum_scatter(bc_part.astype(jnp.bfloat16), "head", scatter_dimension=0, tiled=True)
    norm_scale = (lax.axis_size("seq") * tokens_here * head_dim) ** (-0.5)
    param_grad = lax.psum(param_terms, "seq") * norm_scale
    return (in_part, bc_sum, dt_grad, param_grad)


def solution(mesh):
    return jax.shard_map(
        shards,
        mesh=mesh,
        in_specs=(
            P("seq", "head"),
            P("seq", "head"),
            P("seq", None),
            P("seq", None),
            P("head", "seq"),
            P("head"),
            P("head"),
            P("head"),
            P("seq", "head", None),
            P("head", None),
            P(None, "head"),
        ),
        out_specs=(P("head", "seq"), P("head", "seq"), P("head", "seq"), P(None, "head")),
        check_vma=False,
    )
```

profile of v0, /device:TPU:2, one launch (start us, length us, event | category | flops | bytes accessed | tf_op | source)
XLA Modules:
  0.0 642.7 jit_solution(2640681701304499436)
XLA Ops:
  14.1 103.5 %all-gather.2.cloned.1.call-done = bf16[256,4096]{1,0:T(8,128)(2,1)} async-done(((bf16[256,256]{1,0:T(8,128)(2,1)}), bf16[256,4096]{1,0:T(8,128)(2,1)}) %all-gather.2.cloned.1.call-update) | async-done | bytes 2097168 | tf_op jit(solution)/shard_map/all_gather | solution.py:20
  122.1 276.6 %while.11 = (s32[]{:T(128)}, f32[4,64,128]{2,1,0:T(8,128)S(1)}, f32[4]{0:T(128)S(1)}, f32[4,64,128]{2,1,0:T(8,128)S(1)}, s32[]{:T(128)}) while((s32[]{:T(128)}, f32[4,64,128]{2,1,0:T(8,128)S(1)}, f32[4]{0:T(128)S(1)}, f32[4,64,128]{2,1,0:T(8,128)S(1)}, s32[]{:T(128)}) %tuple.42), condition=%wide.region_3.4_spmd, body=%wide.region_2.3_spmd.sunk | while | flops 65538 | bytes 917621 | solution.py:60
  126.7 6.5 %collective-permute-start = (f32[4,64,128]{2,1,0:T(8,128)S(1)}, f32[4,64,128]{2,1,0:T(8,128)S(1)}, u32[]{:S(2)}, u32[]{:S(2)}) collective-permute-start(f32[4,64,128]{2,1,0:T(8,128)S(1)} %multiply_add_fusion.2), channel_id=1, source_target_pairs={{16,0},{32,16},{48,32},{64,48},{80,64},{96,80},{112,96},{128,112},... | collective-permute-start | bytes 393224 | tf_op jit(solution)/shard_map/while/body/eval_jaxpr/ppermute | solution.py:10
  135.8 6.5 %collective-permute-start = (f32[4,64,128]{2,1,0:T(8,128)S(1)}, f32[4,64,128]{2,1,0:T(8,128)S(1)}, u32[]{:S(2)}, u32[]{:S(2)}) collective-permute-start(f32[4,64,128]{2,1,0:T(8,128)S(1)} %multiply_add_fusion.2), channel_id=1, source_target_pairs={{16,0},{32,16},{48,32},{64,48},{80,64},{96,80},{112,96},{128,112},... | collective-permute-start | bytes 393224 | tf_op jit(solution)/shard_map/while/body/eval_jaxpr/ppermute | solution.py:10
  144.9 6.5 %collective-permute-start = (f32[4,64,128]{2,1,0:T(8,128)S(1)}, f32[4,64,128]{2,1,0:T(8,128)S(1)}, u32[]{:S(2)}, u32[]{:S(2)}) collective-permute-start(f32[4,64,128]{2,1,0:T(8,128)S(1)} %multiply_add_fusion.2), channel_id=1, source_target_pairs={{16,0},{32,16},{48,32},{64,48},{80,64},{96,80},{112,96},{128,112},... | collective-permute-start | bytes 393224 | tf_op jit(solution)/shard_map/while/body/eval_jaxpr/ppermute | solution.py:10
  153.9 6.5 %collective-permute-start = (f32[4,64,128]{2,1,0:T(8,128)S(1)}, f32[4,64,128]{2,1,0:T(8,128)S(1)}, u32[]{:S(2)}, u32[]{:S(2)}) collective-permute-start(f32[4,64,128]{2,1,0:T(8,128)S(1)} %multiply_add_fusion.2), channel_id=1, source_target_pairs={{16,0},{32,16},{48,32},{64,48},{80,64},{96,80},{112,96},{128,112},... | collective-permute-start | bytes 393224 | tf_op jit(solution)/shard_map/while/body/eval_jaxpr/ppermute | solution.py:10
  163.0 6.5 %collective-permute-start = (f32[4,64,128]{2,1,0:T(8,128)S(1)}, f32[4,64,128]{2,1,0:T(8,128)S(1)}, u32[]{:S(2)}, u32[]{:S(2)}) collective-permute-start(f32[4,64,128]{2,1,0:T(8,128)S(1)} %multiply_add_fusion.2), channel_id=1, source_target_pairs={{16,0},{32,16},{48,32},{64,48},{80,64},{96,80},{112,96},{128,112},... | collective-permute-start | bytes 393224 | tf_op jit(solution)/shard_map/while/body/eval_jaxpr/ppermute | solution.py:10
  172.1 6.5 %collective-permute-start = (f32[4,64,128]{2,1,0:T(8,128)S(1)}, f32[4,64,128]{2,1,0:T(8,128)S(1)}, u32[]{:S(2)}, u32[]{:S(2)}) collective-permute-start(f32[4,64,128]{2,1,0:T(8,128)S(1)} %multiply_add_fusion.2), channel_id=1, source_target_pairs={{16,0},{32,16},{48,32},{64,48},{80,64},{96,80},{112,96},{128,112},... | collective-permute-start | bytes 393224 | tf_op jit(solution)/shard_map/while/body/eval_jaxpr/ppermute | solution.py:10
  181.1 6.5 %collective-permute-start = (f32[4,64,128]{2,1,0:T(8,128)S(1)}, f32[4,64,128]{2,1,0:T(8,128)S(1)}, u32[]{:S(2)}, u32[]{:S(2)}) collective-permute-start(f32[4,64,128]{2,1,0:T(8,128)S(1)} %multiply_add_fusion.2), channel_id=1, source_target_pairs={{16,0},{32,16},{48,32},{64,48},{80,64},{96,80},{112,96},{128,112},... | collective-permute-start | bytes 393224 | tf_op jit(solution)/shard_map/while/body/eval_jaxpr/ppermute | solution.py:10
  190.2 6.5 %collective-permute-start = (f32[4,64,128]{2,1,0:T(8,128)S(1)}, f32[4,64,128]{2,1,0:T(8,128)S(1)}, u32[]{:S(2)}, u32[]{:S(2)}) collective-permute-start(f32[4,64,128]{2,1,0:T(8,128)S(1)} %multiply_add_fusion.2), channel_id=1, source_target_pairs={{16,0},{32,16},{48,32},{64,48},{80,64},{96,80},{112,96},{128,112},... | collective-permute-start | bytes 393224 | tf_op jit(solution)/shard_map/while/body/eval_jaxpr/ppermute | solution.py:10
  199.3 6.5 %collective-permute-start = (f32[4,64,128]{2,1,0:T(8,128)S(1)}, f32[4,64,128]{2,1,0:T(8,128)S(1)}, u32[]{:S(2)}, u32[]{:S(2)}) collective-permute-start(f32[4,64,128]{2,1,0:T(8,128)S(1)} %multiply_add_fusion.2), channel_id=1, source_target_pairs={{16,0},{32,16},{48,32},{64,48},{80,64},{96,80},{112,96},{128,112},... | collective-permute-start | bytes 393224 | tf_op jit(solution)/shard_map/while/body/eval_jaxpr/ppermute | solution.py:10
  208.4 6.5 %collective-permute-start = (f32[4,64,128]{2,1,0:T(8,128)S(1)}, f32[4,64,128]{2,1,0:T(8,128)S(1)}, u32[]{:S(2)}, u32[]{:S(2)}) collective-permute-start(f32[4,64,128]{2,1,0:T(8,128)S(1)} %multiply_add_fusion.2), channel_id=1, source_target_pairs={{16,0},{32,16},{48,32},{64,48},{80,64},{96,80},{112,96},{128,112},... | collective-permute-start | bytes 393224 | tf_op jit(solution)/shard_map/while/body/eval_jaxpr/ppermute | solution.py:10
  217.4 6.5 %collective-permute-start = (f32[4,64,128]{2,1,0:T(8,128)S(1)}, f32[4,64,128]{2,1,0:T(8,128)S(1)}, u32[]{:S(2)}, u32[]{:S(2)}) collective-permute-start(f32[4,64,128]{2,1,0:T(8,128)S(1)} %multiply_add_fusion.2), channel_id=1, source_target_pairs={{16,0},{32,16},{48,32},{64,48},{80,64},{96,80},{112,96},{128,112},... | collective-permute-start | bytes 393224 | tf_op jit(solution)/shard_map/while/body/eval_jaxpr/ppermute | solution.py:10
  226.5 6.5 %collective-permute-start = (f32[4,64,128]{2,1,0:T(8,128)S(1)}, f32[4,64,128]{2,1,0:T(8,128)S(1)}, u32[]{:S(2)}, u32[]{:S(2)}) collective-permute-start(f32[4,64,128]{2,1,0:T(8,128)S(1)} %multiply_add_fusion.2), channel_id=1, source_target_pairs={{16,0},{32,16},{48,32},{64,48},{80,64},{96,80},{112,96},{128,112},... | collective-permute-start | bytes 393224 | tf_op jit(solution)/shard_map/while/body/eval_jaxpr/ppermute | solution.py:10
  235.6 6.5 %collective-permute-start = (f32[4,64,128]{2,1,0:T(8,128)S(1)}, f32[4,64,128]{2,1,0:T(8,128)S(1)}, u32[]{:S(2)}, u32[]{:S(2)}) collective-permute-start(f32[4,64,128]{2,1,0:T(8,128)S(1)} %multiply_add_fusion.2), channel_id=1, source_target_pairs={{16,0},{32,16},{48,32},{64,48},{80,64},{96,80},{112,96},{128,112},... | collective-permute-start | bytes 393224 | tf_op jit(solution)/shard_map/while/body/eval_jaxpr/ppermute | solution.py:10
  244.6 6.5 %collective-permute-start = (f32[4,64,128]{2,1,0:T(8,128)S(1)}, f32[4,64,128]{2,1,0:T(8,128)S(1)}, u32[]{:S(2)}, u32[]{:S(2)}) collective-permute-start(f32[4,64,128]{2,1,0:T(8,128)S(1)} %multiply_add_fusion.2), channel_id=1, source_target_pairs={{16,0},{32,16},{48,32},{64,48},{80,64},{96,80},{112,96},{128,112},... | collective-permute-start | bytes 393224 | tf_op jit(solution)/shard_map/while/body/eval_jaxpr/ppermute | solution.py:10
  253.7 6.5 %collective-permute-start = (f32[4,64,128]{2,1,0:T(8,128)S(1)}, f32[4,64,128]{2,1,0:T(8,128)S(1)}, u32[]{:S(2)}, u32[]{:S(2)}) collective-permute-start(f32[4,64,128]{2,1,0:T(8,128)S(1)} %multiply_add_fusion.2), channel_id=1, source_target_pairs={{16,0},{32,16},{48,32},{64,48},{80,64},{96,80},{112,96},{128,112},... | collective-permute-start | bytes 393224 | tf_op jit(solution)/shard_map/while/body/eval_jaxpr/ppermute | solution.py:10
  262.8 6.5 %collective-permute-start = (f32[4,64,128]{2,1,0:T(8,128)S(1)}, f32[4,64,128]{2,1,0:T(8,128)S(1)}, u32[]{:S(2)}, u32[]{:S(2)}) collective-permute-start(f32[4,64,128]{2,1,0:T(8,128)S(1)} %multiply_add_fusion.2), channel_id=1, source_target_pairs={{16,0},{32,16},{48,32},{64,48},{80,64},{96,80},{112,96},{128,112},... | collective-permute-start | bytes 393224 | tf_op jit(solution)/shard_map/while/body/eval_jaxpr/ppermute | solution.py:10
  271.8 6.5 %collective-permute-start = (f32[4,64,128]{2,1,0:T(8,128)S(1)}, f32[4,64,128]{2,1,0:T(8,128)S(1)}, u32[]{:S(2)}, u32[]{:S(2)}) collective-permute-start(f32[4,64,128]{2,1,0:T(8,128)S(1)} %multiply_add_fusion.2), channel_id=1, source_target_pairs={{16,0},{32,16},{48,32},{64,48},{80,64},{96,80},{112,96},{128,112},... | collective-permute-start | bytes 393224 | tf_op jit(solution)/shard_map/while/body/eval_jaxpr/ppermute | solution.py:10
  280.9 6.5 %collective-permute-start = (f32[4,64,128]{2,1,0:T(8,128)S(1)}, f32[4,64,128]{2,1,0:T(8,128)S(1)}, u32[]{:S(2)}, u32[]{:S(2)}) collective-permute-start(f32[4,64,128]{2,1,0:T(8,128)S(1)} %multiply_add_fusion.2), channel_id=1, source_target_pairs={{16,0},{32,16},{48,32},{64,48},{80,64},{96,80},{112,96},{128,112},... | collective-permute-start | bytes 393224 | tf_op jit(solution)/shard_map/while/body/eval_jaxpr/ppermute | solution.py:10
  290.0 6.5 %collective-permute-start = (f32[4,64,128]{2,1,0:T(8,128)S(1)}, f32[4,64,128]{2,1,0:T(8,128)S(1)}, u32[]{:S(2)}, u32[]{:S(2)}) collective-permute-start(f32[4,64,128]{2,1,0:T(8,128)S(1)} %multiply_add_fusion.2), channel_id=1, source_target_pairs={{16,0},{32,16},{48,32},{64,48},{80,64},{96,80},{112,96},{128,112},... | collective-permute-start | bytes 393224 | tf_op jit(solution)/shard_map/while/body/eval_jaxpr/ppermute | solution.py:10
  299.0 6.5 %collective-permute-start = (f32[4,64,128]{2,1,0:T(8,128)S(1)}, f32[4,64,128]{2,1,0:T(8,128)S(1)}, u32[]{:S(2)}, u32[]{:S(2)}) collective-permute-start(f32[4,64,128]{2,1,0:T(8,128)S(1)} %multiply_add_fusion.2), channel_id=1, source_target_pairs={{16,0},{32,16},{48,32},{64,48},{80,64},{96,80},{112,96},{128,112},... | collective-permute-start | bytes 393224 | tf_op jit(solution)/shard_map/while/body/eval_jaxpr/ppermute | solution.py:10
  308.1 6.5 %collective-permute-start = (f32[4,64,128]{2,1,0:T(8,128)S(1)}, f32[4,64,128]{2,1,0:T(8,128)S(1)}, u32[]{:S(2)}, u32[]{:S(2)}) collective-permute-start(f32[4,64,128]{2,1,0:T(8,128)S(1)} %multiply_add_fusion.2), channel_id=1, source_target_pairs={{16,0},{32,16},{48,32},{64,48},{80,64},{96,80},{112,96},{128,112},... | collective-permute-start | bytes 393224 | tf_op jit(solution)/shard_map/while/body/eval_jaxpr/ppermute | solution.py:10
  317.2 6.5 %collective-permute-start = (f32[4,64,128]{2,1,0:T(8,128)S(1)}, f32[4,64,128]{2,1,0:T(8,128)S(1)}, u32[]{:S(2)}, u32[]{:S(2)}) collective-permute-start(f32[4,64,128]{2,1,0:T(8,128)S(1)} %multiply_add_fusion.2), channel_id=1, source_target_pairs={{16,0},{32,16},{48,32},{64,48},{80,64},{96,80},{112,96},{128,112},... | collective-permute-start | bytes 393224 | tf_op jit(solution)/shard_map/while/body/eval_jaxpr/ppermute | solution.py:10
  326.2 6.5 %collective-permute-start = (f32[4,64,128]{2,1,0:T(8,128)S(1)}, f32[4,64,128]{2,1,0:T(8,128)S(1)}, u32[]{:S(2)}, u32[]{:S(2)}) collective-permute-start(f32[4,64,128]{2,1,0:T(8,128)S(1)} %multiply_add_fusion.2), channel_id=1, source_target_pairs={{16,0},{32,16},{48,32},{64,48},{80,64},{96,80},{112,96},{128,112},... | collective-permute-start | bytes 393224 | tf_op jit(solution)/shard_map/while/body/eval_jaxpr/ppermute | solution.py:10
  335.3 6.5 %collective-permute-start = (f32[4,64,128]{2,1,0:T(8,128)S(1)}, f32[4,64,128]{2,1,0:T(8,128)S(1)}, u32[]{:S(2)}, u32[]{:S(2)}) collective-permute-start(f32[4,64,128]{2,1,0:T(8,128)S(1)} %multiply_add_fusion.2), channel_id=1, source_target_pairs={{16,0},{32,16},{48,32},{64,48},{80,64},{96,80},{112,96},{128,112},... | collective-permute-start | bytes 393224 | tf_op jit(solution)/shard_map/while/body/eval_jaxpr/ppermute | solution.py:10
  344.4 6.5 %collective-permute-start = (f32[4,64,128]{2,1,0:T(8,128)S(1)}, f32[4,64,128]{2,1,0:T(8,128)S(1)}, u32[]{:S(2)}, u32[]{:S(2)}) collective-permute-start(f32[4,64,128]{2,1,0:T(8,128)S(1)} %multiply_add_fusion.2), channel_id=1, source_target_pairs={{16,0},{32,16},{48,32},{64,48},{80,64},{96,80},{112,96},{128,112},... | collective-permute-start | bytes 393224 | tf_op jit(solution)/shard_map/while/body/eval_jaxpr/ppermute | solution.py:10
  353.4 6.5 %collective-permute-start = (f32[4,64,128]{2,1,0:T(8,128)S(1)}, f32[4,64,128]{2,1,0:T(8,128)S(1)}, u32[]{:S(2)}, u32[]{:S(2)}) collective-permute-start(f32[4,64,128]{2,1,0:T(8,128)S(1)} %multiply_add_fusion.2), channel_id=1, source_target_pairs={{16,0},{32,16},{48,32},{64,48},{80,64},{96,80},{112,96},{128,112},... | collective-permute-start | bytes 393224 | tf_op jit(solution)/shard_map/while/body/eval_jaxpr/ppermute | solution.py:10
  362.5 6.5 %collective-permute-start = (f32[4,64,128]{2,1,0:T(8,128)S(1)}, f32[4,64,128]{2,1,0:T(8,128)S(1)}, u32[]{:S(2)}, u32[]{:S(2)}) collective-permute-start(f32[4,64,128]{2,1,0:T(8,128)S(1)} %multiply_add_fusion.2), channel_id=1, source_target_pairs={{16,0},{32,16},{48,32},{64,48},{80,64},{96,80},{112,96},{128,112},... | collective-permute-start | bytes 393224 | tf_op jit(solution)/shard_map/while/body/eval_jaxpr/ppermute | solution.py:10
  409.2 65.6 %psum.7 = f32[3,4]{1,0:T(4,128)S(1)} all-reduce(f32[3,4]{1,0:T(4,128)S(1)} %pad_maximum_fusion.1), channel_id=1, replica_groups=mesh['seq'=32,'head'=16] {'seq'}, use_global_device_ids=true, to_apply=%region_20.21 | all-reduce | flops 12 | bytes 96 | tf_op jit(solution)/shard_map/psum | solution.py:102
  475.4 49.7 %reduce-scatter.3.cloned.1.call-done = bf16[256,256]{0,1:T(8,128)(2,1)} async-done(((bf16[4096,256]{0,1:T(8,128)(2,1)}), bf16[256,256]{0,1:T(8,128)(2,1)}) %reduce-scatter.3.cloned.1.call-update) | async-done | bytes 131088 | tf_op jit(solution)/shard_map/reduce_scatter | solution.py:92
  526.7 109.5 %reduce-scatter.5.cloned.1.call-done = bf16[16,256]{1,0:T(8,128)(2,1)} async-done(((bf16[256,256]{1,0:T(8,128)(2,1)}), bf16[16,256]{1,0:T(8,128)(2,1)}) %reduce-scatter.5.cloned.1.call-update) | async-done | bytes 8208 | tf_op jit(solution)/shard_map/reduce_scatter | solution.py:100
  (139 shorter events, 125.1 us)
Async XLA Ops:
  7.2 110.5 %all-gather.2.cloned.1.call-start = ((), (), s32[]{:S(2)}) async-start(), calls=%async_computation.2 | async-start | bytes 2228224 | tf_op jit(solution)/shard_map/all_gather | solution.py:20
  7.9 517.1 %reduce-scatter.3.cloned.1.call-start = ((), (), s32[]{:S(2)}) async-start(), calls=%async_computation.3 | async-start | bytes 2228224 | tf_op jit(solution)/shard_map/reduce_scatter | solution.py:92
  126.7 9.0 %collective-permute-start = (f32[4,64,128]{2,1,0:T(8,128)S(1)}, f32[4,64,128]{2,1,0:T(8,128)S(1)}, u32[]{:S(2)}, u32[]{:S(2)}) collective-permute-start(f32[4,64,128]{2,1,0:T(8,128)S(1)} %multiply_add_fusion.2), channel_id=1, source_target_pairs={{16,0},{32,16},{48,32},{64,48},{80,64},{96,80},{112,96},{128,112},... | collective-permute-start | bytes 393224 | tf_op jit(solution)/shard_map/while/body/eval_jaxpr/ppermute | solution.py:10
  135.8 9.0 %collective-permute-start = (f32[4,64,128]{2,1,0:T(8,128)S(1)}, f32[4,64,128]{2,1,0:T(8,128)S(1)}, u32[]{:S(2)}, u32[]{:S(2)}) collective-permute-start(f32[4,64,128]{2,1,0:T(8,128)S(1)} %multiply_add_fusion.2), channel_id=1, source_target_pairs={{16,0},{32,16},{48,32},{64,48},{80,64},{96,80},{112,96},{128,112},... | collective-permute-start | bytes 393224 | tf_op jit(solution)/shard_map/while/body/eval_jaxpr/ppermute | solution.py:10
  144.9 9.0 %collective-permute-start = (f32[4,64,128]{2,1,0:T(8,128)S(1)}, f32[4,64,128]{2,1,0:T(8,128)S(1)}, u32[]{:S(2)}, u32[]{:S(2)}) collective-permute-start(f32[4,64,128]{2,1,0:T(8,128)S(1)} %multiply_add_fusion.2), channel_id=1, source_target_pairs={{16,0},{32,16},{48,32},{64,48},{80,64},{96,80},{112,96},{128,112},... | collective-permute-start | bytes 393224 | tf_op jit(solution)/shard_map/while/body/eval_jaxpr/ppermute | solution.py:10
  153.9 9.0 %collective-permute-start = (f32[4,64,128]{2,1,0:T(8,128)S(1)}, f32[4,64,128]{2,1,0:T(8,128)S(1)}, u32[]{:S(2)}, u32[]{:S(2)}) collective-permute-start(f32[4,64,128]{2,1,0:T(8,128)S(1)} %multiply_add_fusion.2), channel_id=1, source_target_pairs={{16,0},{32,16},{48,32},{64,48},{80,64},{96,80},{112,96},{128,112},... | collective-permute-start | bytes 393224 | tf_op jit(solution)/shard_map/while/body/eval_jaxpr/ppermute | solution.py:10
  163.0 9.0 %collective-permute-start = (f32[4,64,128]{2,1,0:T(8,128)S(1)}, f32[4,64,128]{2,1,0:T(8,128)S(1)}, u32[]{:S(2)}, u32[]{:S(2)}) collective-permute-start(f32[4,64,128]{2,1,0:T(8,128)S(1)} %multiply_add_fusion.2), channel_id=1, source_target_pairs={{16,0},{32,16},{48,32},{64,48},{80,64},{96,80},{112,96},{128,112},... | collective-permute-start | bytes 393224 | tf_op jit(solution)/shard_map/while/body/eval_jaxpr/ppermute | solution.py:10
  172.1 9.0 %collective-permute-start = (f32[4,64,128]{2,1,0:T(8,128)S(1)}, f32[4,64,128]{2,1,0:T(8,128)S(1)}, u32[]{:S(2)}, u32[]{:S(2)}) collective-permute-start(f32[4,64,128]{2,1,0:T(8,128)S(1)} %multiply_add_fusion.2), channel_id=1, source_target_pairs={{16,0},{32,16},{48,32},{64,48},{80,64},{96,80},{112,96},{128,112},... | collective-permute-start | bytes 393224 | tf_op jit(solution)/shard_map/while/body/eval_jaxpr/ppermute | solution.py:10
  181.1 9.0 %collective-permute-start = (f32[4,64,128]{2,1,0:T(8,128)S(1)}, f32[4,64,128]{2,1,0:T(8,128)S(1)}, u32[]{:S(2)}, u32[]{:S(2)}) collective-permute-start(f32[4,64,128]{2,1,0:T(8,128)S(1)} %multiply_add_fusion.2), channel_id=1, source_target_pairs={{16,0},{32,16},{48,32},{64,48},{80,64},{96,80},{112,96},{128,112},... | collective-permute-start | bytes 393224 | tf_op jit(solution)/shard_map/while/body/eval_jaxpr/ppermute | solution.py:10
  190.2 9.0 %collective-permute-start = (f32[4,64,128]{2,1,0:T(8,128)S(1)}, f32[4,64,128]{2,1,0:T(8,128)S(1)}, u32[]{:S(2)}, u32[]{:S(2)}) collective-permute-start(f32[4,64,128]{2,1,0:T(8,128)S(1)} %multiply_add_fusion.2), channel_id=1, source_target_pairs={{16,0},{32,16},{48,32},{64,48},{80,64},{96,80},{112,96},{128,112},... | collective-permute-start | bytes 393224 | tf_op jit(solution)/shard_map/while/body/eval_jaxpr/ppermute | solution.py:10
  199.3 9.0 %collective-permute-start = (f32[4,64,128]{2,1,0:T(8,128)S(1)}, f32[4,64,128]{2,1,0:T(8,128)S(1)}, u32[]{:S(2)}, u32[]{:S(2)}) collective-permute-start(f32[4,64,128]{2,1,0:T(8,128)S(1)} %multiply_add_fusion.2), channel_id=1, source_target_pairs={{16,0},{32,16},{48,32},{64,48},{80,64},{96,80},{112,96},{128,112},... | collective-permute-start | bytes 393224 | tf_op jit(solution)/shard_map/while/body/eval_jaxpr/ppermute | solution.py:10
  208.4 9.0 %collective-permute-start = (f32[4,64,128]{2,1,0:T(8,128)S(1)}, f32[4,64,128]{2,1,0:T(8,128)S(1)}, u32[]{:S(2)}, u32[]{:S(2)}) collective-permute-start(f32[4,64,128]{2,1,0:T(8,128)S(1)} %multiply_add_fusion.2), channel_id=1, source_target_pairs={{16,0},{32,16},{48,32},{64,48},{80,64},{96,80},{112,96},{128,112},... | collective-permute-start | bytes 393224 | tf_op jit(solution)/shard_map/while/body/eval_jaxpr/ppermute | solution.py:10
  217.4 9.0 %collective-permute-start = (f32[4,64,128]{2,1,0:T(8,128)S(1)}, f32[4,64,128]{2,1,0:T(8,128)S(1)}, u32[]{:S(2)}, u32[]{:S(2)}) collective-permute-start(f32[4,64,128]{2,1,0:T(8,128)S(1)} %multiply_add_fusion.2), channel_id=1, source_target_pairs={{16,0},{32,16},{48,32},{64,48},{80,64},{96,80},{112,96},{128,112},... | collective-permute-start | bytes 393224 | tf_op jit(solution)/shard_map/while/body/eval_jaxpr/ppermute | solution.py:10
  226.5 9.0 %collective-permute-start = (f32[4,64,128]{2,1,0:T(8,128)S(1)}, f32[4,64,128]{2,1,0:T(8,128)S(1)}, u32[]{:S(2)}, u32[]{:S(2)}) collective-permute-start(f32[4,64,128]{2,1,0:T(8,128)S(1)} %multiply_add_fusion.2), channel_id=1, source_target_pairs={{16,0},{32,16},{48,32},{64,48},{80,64},{96,80},{112,96},{128,112},... | collective-permute-start | bytes 393224 | tf_op jit(solution)/shard_map/while/body/eval_jaxpr/ppermute | solution.py:10
  235.6 9.0 %collective-permute-start = (f32[4,64,128]{2,1,0:T(8,128)S(1)}, f32[4,64,128]{2,1,0:T(8,128)S(1)}, u32[]{:S(2)}, u32[]{:S(2)}) collective-permute-start(f32[4,64,128]{2,1,0:T(8,128)S(1)} %multiply_add_fusion.2), channel_id=1, source_target_pairs={{16,0},{32,16},{48,32},{64,48},{80,64},{96,80},{112,96},{128,112},... | collective-permute-start | bytes 393224 | tf_op jit(solution)/shard_map/while/body/eval_jaxpr/ppermute | solution.py:10
  244.6 9.0 %collective-permute-start = (f32[4,64,128]{2,1,0:T(8,128)S(1)}, f32[4,64,128]{2,1,0:T(8,128)S(1)}, u32[]{:S(2)}, u32[]{:S(2)}) collective-permute-start(f32[4,64,128]{2,1,0:T(8,128)S(1)} %multiply_add_fusion.2), channel_id=1, source_target_pairs={{16,0},{32,16},{48,32},{64,48},{80,64},{96,80},{112,96},{128,112},... | collective-permute-start | bytes 393224 | tf_op jit(solution)/shard_map/while/body/eval_jaxpr/ppermute | solution.py:10
  253.7 9.0 %collective-permute-start = (f32[4,64,128]{2,1,0:T(8,128)S(1)}, f32[4,64,128]{2,1,0:T(8,128)S(1)}, u32[]{:S(2)}, u32[]{:S(2)}) collective-permute-start(f32[4,64,128]{2,1,0:T(8,128)S(1)} %multiply_add_fusion.2), channel_id=1, source_target_pairs={{16,0},{32,16},{48,32},{64,48},{80,64},{96,80},{112,96},{128,112},... | collective-permute-start | bytes 393224 | tf_op jit(solution)/shard_map/while/body/eval_jaxpr/ppermute | solution.py:10
  262.8 9.0 %collective-permute-start = (f32[4,64,128]{2,1,0:T(8,128)S(1)}, f32[4,64,128]{2,1,0:T(8,128)S(1)}, u32[]{:S(2)}, u32[]{:S(2)}) collective-permute-start(f32[4,64,128]{2,1,0:T(8,128)S(1)} %multiply_add_fusion.2), channel_id=1, source_target_pairs={{16,0},{32,16},{48,32},{64,48},{80,64},{96,80},{112,96},{128,112},... | collective-permute-start | bytes 393224 | tf_op jit(solution)/shard_map/while/body/eval_jaxpr/ppermute | solution.py:10
  271.8 9.0 %collective-permute-start = (f32[4,64,128]{2,1,0:T(8,128)S(1)}, f32[4,64,128]{2,1,0:T(8,128)S(1)}, u32[]{:S(2)}, u32[]{:S(2)}) collective-permute-start(f32[4,64,128]{2,1,0:T(8,128)S(1)} %multiply_add_fusion.2), channel_id=1, source_target_pairs={{16,0},{32,16},{48,32},{64,48},{80,64},{96,80},{112,96},{128,112},... | collective-permute-start | bytes 393224 | tf_op jit(solution)/shard_map/while/body/eval_jaxpr/ppermute | solution.py:10
  280.9 9.0 %collective-permute-start = (f32[4,64,128]{2,1,0:T(8,128)S(1)}, f32[4,64,128]{2,1,0:T(8,128)S(1)}, u32[]{:S(2)}, u32[]{:S(2)}) collective-permute-start(f32[4,64,128]{2,1,0:T(8,128)S(1)} %multiply_add_fusion.2), channel_id=1, source_target_pairs={{16,0},{32,16},{48,32},{64,48},{80,64},{96,80},{112,96},{128,112},... | collective-permute-start | bytes 393224 | tf_op jit(solution)/shard_map/while/body/eval_jaxpr/ppermute | solution.py:10
  290.0 9.0 %collective-permute-start = (f32[4,64,128]{2,1,0:T(8,128)S(1)}, f32[4,64,128]{2,1,0:T(8,128)S(1)}, u32[]{:S(2)}, u32[]{:S(2)}) collective-permute-start(f32[4,64,128]{2,1,0:T(8,128)S(1)} %multiply_add_fusion.2), channel_id=1, source_target_pairs={{16,0},{32,16},{48,32},{64,48},{80,64},{96,80},{112,96},{128,112},... | collective-permute-start | bytes 393224 | tf_op jit(solution)/shard_map/while/body/eval_jaxpr/ppermute | solution.py:10
  299.0 9.0 %collective-permute-start = (f32[4,64,128]{2,1,0:T(8,128)S(1)}, f32[4,64,128]{2,1,0:T(8,128)S(1)}, u32[]{:S(2)}, u32[]{:S(2)}) collective-permute-start(f32[4,64,128]{2,1,0:T(8,128)S(1)} %multiply_add_fusion.2), channel_id=1, source_target_pairs={{16,0},{32,16},{48,32},{64,48},{80,64},{96,80},{112,96},{128,112},... | collective-permute-start | bytes 393224 | tf_op jit(solution)/shard_map/while/body/eval_jaxpr/ppermute | solution.py:10
  308.1 9.0 %collective-permute-start = (f32[4,64,128]{2,1,0:T(8,128)S(1)}, f32[4,64,128]{2,1,0:T(8,128)S(1)}, u32[]{:S(2)}, u32[]{:S(2)}) collective-permute-start(f32[4,64,128]{2,1,0:T(8,128)S(1)} %multiply_add_fusion.2), channel_id=1, source_target_pairs={{16,0},{32,16},{48,32},{64,48},{80,64},{96,80},{112,96},{128,112},... | collective-permute-start | bytes 393224 | tf_op jit(solution)/shard_map/while/body/eval_jaxpr/ppermute | solution.py:10
  317.2 9.0 %collective-permute-start = (f32[4,64,128]{2,1,0:T(8,128)S(1)}, f32[4,64,128]{2,1,0:T(8,128)S(1)}, u32[]{:S(2)}, u32[]{:S(2)}) collective-permute-start(f32[4,64,128]{2,1,0:T(8,128)S(1)} %multiply_add_fusion.2), channel_id=1, source_target_pairs={{16,0},{32,16},{48,32},{64,48},{80,64},{96,80},{112,96},{128,112},... | collective-permute-start | bytes 393224 | tf_op jit(solution)/shard_map/while/body/eval_jaxpr/ppermute | solution.py:10
  326.2 9.0 %collective-permute-start = (f32[4,64,128]{2,1,0:T(8,128)S(1)}, f32[4,64,128]{2,1,0:T(8,128)S(1)}, u32[]{:S(2)}, u32[]{:S(2)}) collective-permute-start(f32[4,64,128]{2,1,0:T(8,128)S(1)} %multiply_add_fusion.2), channel_id=1, source_target_pairs={{16,0},{32,16},{48,32},{64,48},{80,64},{96,80},{112,96},{128,112},... | collective-permute-start | bytes 393224 | tf_op jit(solution)/shard_map/while/body/eval_jaxpr/ppermute | solution.py:10
  335.3 9.0 %collective-permute-start = (f32[4,64,128]{2,1,0:T(8,128)S(1)}, f32[4,64,128]{2,1,0:T(8,128)S(1)}, u32[]{:S(2)}, u32[]{:S(2)}) collective-permute-start(f32[4,64,128]{2,1,0:T(8,128)S(1)} %multiply_add_fusion.2), channel_id=1, source_target_pairs={{16,0},{32,16},{48,32},{64,48},{80,64},{96,80},{112,96},{128,112},... | collective-permute-start | bytes 393224 | tf_op jit(solution)/shard_map/while/body/eval_jaxpr/ppermute | solution.py:10
  344.4 9.0 %collective-permute-start = (f32[4,64,128]{2,1,0:T(8,128)S(1)}, f32[4,64,128]{2,1,0:T(8,128)S(1)}, u32[]{:S(2)}, u32[]{:S(2)}) collective-permute-start(f32[4,64,128]{2,1,0:T(8,128)S(1)} %multiply_add_fusion.2), channel_id=1, source_target_pairs={{16,0},{32,16},{48,32},{64,48},{80,64},{96,80},{112,96},{128,112},... | collective-permute-start | bytes 393224 | tf_op jit(solution)/shard_map/while/body/eval_jaxpr/ppermute | solution.py:10
  353.4 9.0 %collective-permute-start = (f32[4,64,128]{2,1,0:T(8,128)S(1)}, f32[4,64,128]{2,1,0:T(8,128)S(1)}, u32[]{:S(2)}, u32[]{:S(2)}) collective-permute-start(f32[4,64,128]{2,1,0:T(8,128)S(1)} %multiply_add_fusion.2), channel_id=1, source_target_pairs={{16,0},{32,16},{48,32},{64,48},{80,64},{96,80},{112,96},{128,112},... | collective-permute-start | bytes 393224 | tf_op jit(solution)/shard_map/while/body/eval_jaxpr/ppermute | solution.py:10
  362.5 9.0 %collective-permute-start = (f32[4,64,128]{2,1,0:T(8,128)S(1)}, f32[4,64,128]{2,1,0:T(8,128)S(1)}, u32[]{:S(2)}, u32[]{:S(2)}) collective-permute-start(f32[4,64,128]{2,1,0:T(8,128)S(1)} %multiply_add_fusion.2), channel_id=1, source_target_pairs={{16,0},{32,16},{48,32},{64,48},{80,64},{96,80},{112,96},{128,112},... | collective-permute-start | bytes 393224 | tf_op jit(solution)/shard_map/while/body/eval_jaxpr/ppermute | solution.py:10
  380.6 9.0 %collective-permute-start = (f32[4,64,128]{2,1,0:T(8,128)S(1)}, f32[4,64,128]{2,1,0:T(8,128)S(1)}, u32[]{:S(2)}, u32[]{:S(2)}) collective-permute-start(f32[4,64,128]{2,1,0:T(8,128)S(1)} %multiply_add_fusion.2), channel_id=1, source_target_pairs={{16,0},{32,16},{48,32},{64,48},{80,64},{96,80},{112,96},{128,112},... | collective-permute-start | bytes 393224 | tf_op jit(solution)/shard_map/while/body/eval_jaxpr/ppermute | solution.py:10
  389.7 9.0 %collective-permute-start = (f32[4,64,128]{2,1,0:T(8,128)S(1)}, f32[4,64,128]{2,1,0:T(8,128)S(1)}, u32[]{:S(2)}, u32[]{:S(2)}) collective-permute-start(f32[4,64,128]{2,1,0:T(8,128)S(1)} %multiply_add_fusion.2), channel_id=1, source_target_pairs={{16,0},{32,16},{48,32},{64,48},{80,64},{96,80},{112,96},{128,112},... | collective-permute-start | bytes 393224 | tf_op jit(solution)/shard_map/while/body/eval_jaxpr/ppermute | solution.py:10
  402.1 234.1 %reduce-scatter.5.cloned.1.call-start = ((), (), s32[]{:S(2)}) async-start(), calls=%async_computation.4 | async-start | bytes 139264 | tf_op jit(solution)/shard_map/reduce_scatter | solution.py:100
  (9 other events, 969.1 us)
Sparse Core Ops, SparseCore 0:
  11.0 106.6 all-gather.1
  402.2 122.7 reduce-scatter.2
  530.2 105.9 reduce-scatter.4
where the time goes:
time: 644 us; the launch traced here: 643 us
  waiting for transfers between devices  341 us (53%)
  starting transfers between devices  196 us (30%)
  blocking collectives  65.6 us (10%)
  between operations  13.9 us (2%)
  matrix products  10.6 us (2%)
  other arithmetic  9.97 us (2%)
    ppermute x31, starting transfers between devices, passed_along(): lax.ppermute(value, axis, [(source, source + steps) for source in range(i...  196 us
    reduce_scatter x1, waiting for transfers between devices, shards(): lax.psum_scatter(bc_part.astype(jnp.bfloat16), 'head', scatter_dimension=...  110 us
    all_gather x1, waiting for transfers between devices, shards(): lax.all_gather(out_grad, 'head', axis=1, tiled=True)  104 us
    ppermute x31, waiting for transfers between devices, passed_along(): lax.ppermute(value, axis, [(source, source + steps) for source in range(i...  77.4 us
    psum x1, blocking collectives, shards(): param_grad = lax.psum(param_terms, 'seq') * norm_scale  65.6 us
    reduce_scatter x1, waiting for transfers between devices, shards(): lax.psum_scatter(lax.dot_general(w_in, x_grad, contract_last, preferred_e...  49.7 us
  transfers between devices with their start and end apart: 34, of which 34 were waited for; matrix products, arithmetic and copies ran while one was open for 2% of the time, Pallas kernels for 0%

commit v1 on v0

--- a/solution.py
+++ b/solution.py
@@ -99,7 +99,7 @@
     )
     bc_sum = lax.psum_scatter(bc_part.astype(jnp.bfloat16), "head", scatter_dimension=0, tiled=True)
     norm_scale = (lax.axis_size("seq") * tokens_here * head_dim) ** (-0.5)
-    param_grad = lax.psum(param_terms, "seq") * norm_scale
+    param_grad = jnp.sum(lax.all_gather(param_terms, "seq"), axis=0) * norm_scale
     return (in_part, bc_sum, dt_grad, param_grad)
 
 

time: 644 us -> 645 us (level)
  waiting for transfers between devices: 341 us -> 374 us
  blocking collectives: 65.6 us -> 33.6 us
    psum x1 -> x0, blocking collectives: 65.6 us -> none  [shards(): param_grad = lax.psum(param_terms, 'seq') * norm_scale]
    all_gather x0 -> x1, blocking collectives: none -> 33.6 us  [shards(): lax.all_gather(param_terms, 'seq')]
    reduce_scatter x1, waiting for transfers between devices: 49.7 us -> 82.9 us  [shards(): lax.psum_scatter(lax.dot_general(w_in, x_grad, contract_last, preferred_e...]
where the time goes in v1:
time: 645 us; the launch traced here: 644 us
  waiting for transfers between devices  374 us (58%)
  starting transfers between devices  196 us (30%)
  blocking collectives  33.6 us (5%)
  between operations  13.9 us (2%)
  matrix products  10.6 us (2%)
  other arithmetic  10 us (2%)
    ppermute x31, starting transfers between devices, passed_along(): lax.ppermute(value, axis, [(source, source + steps) for source in range(i...  196 us
    reduce_scatter x1, waiting for transfers between devices, shards(): lax.psum_scatter(bc_part.astype(jnp.bfloat16), 'head', scatter_dimension=...  109 us
    all_gather x1, waiting for transfers between devices, shards(): lax.all_gather(out_grad, 'head', axis=1, tiled=True)  104 us
    reduce_scatter x1, waiting for transfers between devices, shards(): lax.psum_scatter(lax.dot_general(w_in, x_grad, contract_last, preferred_e...  82.9 us
    ppermute x31, waiting for transfers between devices, passed_along(): lax.ppermute(value, axis, [(source, source + steps) for source in range(i...  77.4 us
    all_gather x1, blocking collectives, shards(): lax.all_gather(param_terms, 'seq')  33.6 us
  transfers between devices with their start and end apart: 34, of which 34 were waited for; matrix products, arithmetic and copies ran while one was open for 2% of the time, Pallas kernels for 0%

profile of v1, /device:TPU:2, one launch (start us, length us, event | category | flops | bytes accessed | tf_op | source)
XLA Modules:
  0.0 643.8 jit_solution(12040905796813344732)
XLA Ops:
  14.1 103.5 %all-gather.4.cloned.1.call-done = bf16[256,4096]{1,0:T(8,128)(2,1)} async-done(((bf16[256,256]{1,0:T(8,128)(2,1)}), bf16[256,4096]{1,0:T(8,128)(2,1)}) %all-gather.4.cloned.1.call-update) | async-done | bytes 2097168 | tf_op jit(solution)/shard_map/all_gather | solution.py:20
  122.1 276.6 %while.11 = (s32[]{:T(128)}, f32[4,64,128]{2,1,0:T(8,128)S(1)}, f32[4]{0:T(128)S(1)}, f32[4,64,128]{2,1,0:T(8,128)S(1)}, s32[]{:T(128)}) while((s32[]{:T(128)}, f32[4,64,128]{2,1,0:T(8,128)S(1)}, f32[4]{0:T(128)S(1)}, f32[4,64,128]{2,1,0:T(8,128)S(1)}, s32[]{:T(128)}) %tuple.42), condition=%wide.region_3.4_spmd, body=%wide.region_2.3_spmd.sunk | while | flops 65538 | bytes 917621 | solution.py:60
  126.7 6.5 %collective-permute-start = (f32[4,64,128]{2,1,0:T(8,128)S(1)}, f32[4,64,128]{2,1,0:T(8,128)S(1)}, u32[]{:S(2)}, u32[]{:S(2)}) collective-permute-start(f32[4,64,128]{2,1,0:T(8,128)S(1)} %multiply_add_fusion.2), channel_id=1, source_target_pairs={{16,0},{32,16},{48,32},{64,48},{80,64},{96,80},{112,96},{128,112},... | collective-permute-start | bytes 393224 | tf_op jit(solution)/shard_map/while/body/eval_jaxpr/ppermute | solution.py:10
  135.8 6.5 %collective-permute-start = (f32[4,64,128]{2,1,0:T(8,128)S(1)}, f32[4,64,128]{2,1,0:T(8,128)S(1)}, u32[]{:S(2)}, u32[]{:S(2)}) collective-permute-start(f32[4,64,128]{2,1,0:T(8,128)S(1)} %multiply_add_fusion.2), channel_id=1, source_target_pairs={{16,0},{32,16},{48,32},{64,48},{80,64},{96,80},{112,96},{128,112},... | collective-permute-start | bytes 393224 | tf_op jit(solution)/shard_map/while/body/eval_jaxpr/ppermute | solution.py:10
  144.9 6.5 %collective-permute-start = (f32[4,64,128]{2,1,0:T(8,128)S(1)}, f32[4,64,128]{2,1,0:T(8,128)S(1)}, u32[]{:S(2)}, u32[]{:S(2)}) collective-permute-start(f32[4,64,128]{2,1,0:T(8,128)S(1)} %multiply_add_fusion.2), channel_id=1, source_target_pairs={{16,0},{32,16},{48,32},{64,48},{80,64},{96,80},{112,96},{128,112},... | collective-permute-start | bytes 393224 | tf_op jit(solution)/shard_map/while/body/eval_jaxpr/ppermute | solution.py:10
  153.9 6.5 %collective-permute-start = (f32[4,64,128]{2,1,0:T(8,128)S(1)}, f32[4,64,128]{2,1,0:T(8,128)S(1)}, u32[]{:S(2)}, u32[]{:S(2)}) collective-permute-start(f32[4,64,128]{2,1,0:T(8,128)S(1)} %multiply_add_fusion.2), channel_id=1, source_target_pairs={{16,0},{32,16},{48,32},{64,48},{80,64},{96,80},{112,96},{128,112},... | collective-permute-start | bytes 393224 | tf_op jit(solution)/shard_map/while/body/eval_jaxpr/ppermute | solution.py:10
  163.0 6.5 %collective-permute-start = (f32[4,64,128]{2,1,0:T(8,128)S(1)}, f32[4,64,128]{2,1,0:T(8,128)S(1)}, u32[]{:S(2)}, u32[]{:S(2)}) collective-permute-start(f32[4,64,128]{2,1,0:T(8,128)S(1)} %multiply_add_fusion.2), channel_id=1, source_target_pairs={{16,0},{32,16},{48,32},{64,48},{80,64},{96,80},{112,96},{128,112},... | collective-permute-start | bytes 393224 | tf_op jit(solution)/shard_map/while/body/eval_jaxpr/ppermute | solution.py:10
  172.1 6.5 %collective-permute-start = (f32[4,64,128]{2,1,0:T(8,128)S(1)}, f32[4,64,128]{2,1,0:T(8,128)S(1)}, u32[]{:S(2)}, u32[]{:S(2)}) collective-permute-start(f32[4,64,128]{2,1,0:T(8,128)S(1)} %multiply_add_fusion.2), channel_id=1, source_target_pairs={{16,0},{32,16},{48,32},{64,48},{80,64},{96,80},{112,96},{128,112},... | collective-permute-start | bytes 393224 | tf_op jit(solution)/shard_map/while/body/eval_jaxpr/ppermute | solution.py:10
  181.1 6.5 %collective-permute-start = (f32[4,64,128]{2,1,0:T(8,128)S(1)}, f32[4,64,128]{2,1,0:T(8,128)S(1)}, u32[]{:S(2)}, u32[]{:S(2)}) collective-permute-start(f32[4,64,128]{2,1,0:T(8,128)S(1)} %multiply_add_fusion.2), channel_id=1, source_target_pairs={{16,0},{32,16},{48,32},{64,48},{80,64},{96,80},{112,96},{128,112},... | collective-permute-start | bytes 393224 | tf_op jit(solution)/shard_map/while/body/eval_jaxpr/ppermute | solution.py:10
  190.2 6.5 %collective-permute-start = (f32[4,64,128]{2,1,0:T(8,128)S(1)}, f32[4,64,128]{2,1,0:T(8,128)S(1)}, u32[]{:S(2)}, u32[]{:S(2)}) collective-permute-start(f32[4,64,128]{2,1,0:T(8,128)S(1)} %multiply_add_fusion.2), channel_id=1, source_target_pairs={{16,0},{32,16},{48,32},{64,48},{80,64},{96,80},{112,96},{128,112},... | collective-permute-start | bytes 393224 | tf_op jit(solution)/shard_map/while/body/eval_jaxpr/ppermute | solution.py:10
  199.3 6.5 %collective-permute-start = (f32[4,64,128]{2,1,0:T(8,128)S(1)}, f32[4,64,128]{2,1,0:T(8,128)S(1)}, u32[]{:S(2)}, u32[]{:S(2)}) collective-permute-start(f32[4,64,128]{2,1,0:T(8,128)S(1)} %multiply_add_fusion.2), channel_id=1, source_target_pairs={{16,0},{32,16},{48,32},{64,48},{80,64},{96,80},{112,96},{128,112},... | collective-permute-start | bytes 393224 | tf_op jit(solution)/shard_map/while/body/eval_jaxpr/ppermute | solution.py:10
  208.4 6.5 %collective-permute-start = (f32[4,64,128]{2,1,0:T(8,128)S(1)}, f32[4,64,128]{2,1,0:T(8,128)S(1)}, u32[]{:S(2)}, u32[]{:S(2)}) collective-permute-start(f32[4,64,128]{2,1,0:T(8,128)S(1)} %multiply_add_fusion.2), channel_id=1, source_target_pairs={{16,0},{32,16},{48,32},{64,48},{80,64},{96,80},{112,96},{128,112},... | collective-permute-start | bytes 393224 | tf_op jit(solution)/shard_map/while/body/eval_jaxpr/ppermute | solution.py:10
  217.4 6.5 %collective-permute-start = (f32[4,64,128]{2,1,0:T(8,128)S(1)}, f32[4,64,128]{2,1,0:T(8,128)S(1)}, u32[]{:S(2)}, u32[]{:S(2)}) collective-permute-start(f32[4,64,128]{2,1,0:T(8,128)S(1)} %multiply_add_fusion.2), channel_id=1, source_target_pairs={{16,0},{32,16},{48,32},{64,48},{80,64},{96,80},{112,96},{128,112},... | collective-permute-start | bytes 393224 | tf_op jit(solution)/shard_map/while/body/eval_jaxpr/ppermute | solution.py:10
  226.5 6.5 %collective-permute-start = (f32[4,64,128]{2,1,0:T(8,128)S(1)}, f32[4,64,128]{2,1,0:T(8,128)S(1)}, u32[]{:S(2)}, u32[]{:S(2)}) collective-permute-start(f32[4,64,128]{2,1,0:T(8,128)S(1)} %multiply_add_fusion.2), channel_id=1, source_target_pairs={{16,0},{32,16},{48,32},{64,48},{80,64},{96,80},{112,96},{128,112},... | collective-permute-start | bytes 393224 | tf_op jit(solution)/shard_map/while/body/eval_jaxpr/ppermute | solution.py:10
  235.6 6.5 %collective-permute-start = (f32[4,64,128]{2,1,0:T(8,128)S(1)}, f32[4,64,128]{2,1,0:T(8,128)S(1)}, u32[]{:S(2)}, u32[]{:S(2)}) collective-permute-start(f32[4,64,128]{2,1,0:T(8,128)S(1)} %multiply_add_fusion.2), channel_id=1, source_target_pairs={{16,0},{32,16},{48,32},{64,48},{80,64},{96,80},{112,96},{128,112},... | collective-permute-start | bytes 393224 | tf_op jit(solution)/shard_map/while/body/eval_jaxpr/ppermute | solution.py:10
  244.6 6.5 %collective-permute-start = (f32[4,64,128]{2,1,0:T(8,128)S(1)}, f32[4,64,128]{2,1,0:T(8,128)S(1)}, u32[]{:S(2)}, u32[]{:S(2)}) collective-permute-start(f32[4,64,128]{2,1,0:T(8,128)S(1)} %multiply_add_fusion.2), channel_id=1, source_target_pairs={{16,0},{32,16},{48,32},{64,48},{80,64},{96,80},{112,96},{128,112},... | collective-permute-start | bytes 393224 | tf_op jit(solution)/shard_map/while/body/eval_jaxpr/ppermute | solution.py:10
  253.7 6.5 %collective-permute-start = (f32[4,64,128]{2,1,0:T(8,128)S(1)}, f32[4,64,128]{2,1,0:T(8,128)S(1)}, u32[]{:S(2)}, u32[]{:S(2)}) collective-permute-start(f32[4,64,128]{2,1,0:T(8,128)S(1)} %multiply_add_fusion.2), channel_id=1, source_target_pairs={{16,0},{32,16},{48,32},{64,48},{80,64},{96,80},{112,96},{128,112},... | collective-permute-start | bytes 393224 | tf_op jit(solution)/shard_map/while/body/eval_jaxpr/ppermute | solution.py:10
  262.8 6.5 %collective-permute-start = (f32[4,64,128]{2,1,0:T(8,128)S(1)}, f32[4,64,128]{2,1,0:T(8,128)S(1)}, u32[]{:S(2)}, u32[]{:S(2)}) collective-permute-start(f32[4,64,128]{2,1,0:T(8,128)S(1)} %multiply_add_fusion.2), channel_id=1, source_target_pairs={{16,0},{32,16},{48,32},{64,48},{80,64},{96,80},{112,96},{128,112},... | collective-permute-start | bytes 393224 | tf_op jit(solution)/shard_map/while/body/eval_jaxpr/ppermute | solution.py:10
  271.8 6.5 %collective-permute-start = (f32[4,64,128]{2,1,0:T(8,128)S(1)}, f32[4,64,128]{2,1,0:T(8,128)S(1)}, u32[]{:S(2)}, u32[]{:S(2)}) collective-permute-start(f32[4,64,128]{2,1,0:T(8,128)S(1)} %multiply_add_fusion.2), channel_id=1, source_target_pairs={{16,0},{32,16},{48,32},{64,48},{80,64},{96,80},{112,96},{128,112},... | collective-permute-start | bytes 393224 | tf_op jit(solution)/shard_map/while/body/eval_jaxpr/ppermute | solution.py:10
  280.9 6.5 %collective-permute-start = (f32[4,64,128]{2,1,0:T(8,128)S(1)}, f32[4,64,128]{2,1,0:T(8,128)S(1)}, u32[]{:S(2)}, u32[]{:S(2)}) collective-permute-start(f32[4,64,128]{2,1,0:T(8,128)S(1)} %multiply_add_fusion.2), channel_id=1, source_target_pairs={{16,0},{32,16},{48,32},{64,48},{80,64},{96,80},{112,96},{128,112},... | collective-permute-start | bytes 393224 | tf_op jit(solution)/shard_map/while/body/eval_jaxpr/ppermute | solution.py:10
  290.0 6.5 %collective-permute-start = (f32[4,64,128]{2,1,0:T(8,128)S(1)}, f32[4,64,128]{2,1,0:T(8,128)S(1)}, u32[]{:S(2)}, u32[]{:S(2)}) collective-permute-start(f32[4,64,128]{2,1,0:T(8,128)S(1)} %multiply_add_fusion.2), channel_id=1, source_target_pairs={{16,0},{32,16},{48,32},{64,48},{80,64},{96,80},{112,96},{128,112},... | collective-permute-start | bytes 393224 | tf_op jit(solution)/shard_map/while/body/eval_jaxpr/ppermute | solution.py:10
  299.0 6.5 %collective-permute-start = (f32[4,64,128]{2,1,0:T(8,128)S(1)}, f32[4,64,128]{2,1,0:T(8,128)S(1)}, u32[]{:S(2)}, u32[]{:S(2)}) collective-permute-start(f32[4,64,128]{2,1,0:T(8,128)S(1)} %multiply_add_fusion.2), channel_id=1, source_target_pairs={{16,0},{32,16},{48,32},{64,48},{80,64},{96,80},{112,96},{128,112},... | collective-permute-start | bytes 393224 | tf_op jit(solution)/shard_map/while/body/eval_jaxpr/ppermute | solution.py:10
  308.1 6.5 %collective-permute-start = (f32[4,64,128]{2,1,0:T(8,128)S(1)}, f32[4,64,128]{2,1,0:T(8,128)S(1)}, u32[]{:S(2)}, u32[]{:S(2)}) collective-permute-start(f32[4,64,128]{2,1,0:T(8,128)S(1)} %multiply_add_fusion.2), channel_id=1, source_target_pairs={{16,0},{32,16},{48,32},{64,48},{80,64},{96,80},{112,96},{128,112},... | collective-permute-start | bytes 393224 | tf_op jit(solution)/shard_map/while/body/eval_jaxpr/ppermute | solution.py:10
  317.2 6.5 %collective-permute-start = (f32[4,64,128]{2,1,0:T(8,128)S(1)}, f32[4,64,128]{2,1,0:T(8,128)S(1)}, u32[]{:S(2)}, u32[]{:S(2)}) collective-permute-start(f32[4,64,128]{2,1,0:T(8,128)S(1)} %multiply_add_fusion.2), channel_id=1, source_target_pairs={{16,0},{32,16},{48,32},{64,48},{80,64},{96,80},{112,96},{128,112},... | collective-permute-start | bytes 393224 | tf_op jit(solution)/shard_map/while/body/eval_jaxpr/ppermute | solution.py:10
  326.2 6.5 %collective-permute-start = (f32[4,64,128]{2,1,0:T(8,128)S(1)}, f32[4,64,128]{2,1,0:T(8,128)S(1)}, u32[]{:S(2)}, u32[]{:S(2)}) collective-permute-start(f32[4,64,128]{2,1,0:T(8,128)S(1)} %multiply_add_fusion.2), channel_id=1, source_target_pairs={{16,0},{32,16},{48,32},{64,48},{80,64},{96,80},{112,96},{128,112},... | collective-permute-start | bytes 393224 | tf_op jit(solution)/shard_map/while/body/eval_jaxpr/ppermute | solution.py:10
  335.3 6.5 %collective-permute-start = (f32[4,64,128]{2,1,0:T(8,128)S(1)}, f32[4,64,128]{2,1,0:T(8,128)S(1)}, u32[]{:S(2)}, u32[]{:S(2)}) collective-permute-start(f32[4,64,128]{2,1,0:T(8,128)S(1)} %multiply_add_fusion.2), channel_id=1, source_target_pairs={{16,0},{32,16},{48,32},{64,48},{80,64},{96,80},{112,96},{128,112},... | collective-permute-start | bytes 393224 | tf_op jit(solution)/shard_map/while/body/eval_jaxpr/ppermute | solution.py:10
  344.4 6.5 %collective-permute-start = (f32[4,64,128]{2,1,0:T(8,128)S(1)}, f32[4,64,128]{2,1,0:T(8,128)S(1)}, u32[]{:S(2)}, u32[]{:S(2)}) collective-permute-start(f32[4,64,128]{2,1,0:T(8,128)S(1)} %multiply_add_fusion.2), channel_id=1, source_target_pairs={{16,0},{32,16},{48,32},{64,48},{80,64},{96,80},{112,96},{128,112},... | collective-permute-start | bytes 393224 | tf_op jit(solution)/shard_map/while/body/eval_jaxpr/ppermute | solution.py:10
  353.4 6.5 %collective-permute-start = (f32[4,64,128]{2,1,0:T(8,128)S(1)}, f32[4,64,128]{2,1,0:T(8,128)S(1)}, u32[]{:S(2)}, u32[]{:S(2)}) collective-permute-start(f32[4,64,128]{2,1,0:T(8,128)S(1)} %multiply_add_fusion.2), channel_id=1, source_target_pairs={{16,0},{32,16},{48,32},{64,48},{80,64},{96,80},{112,96},{128,112},... | collective-permute-start | bytes 393224 | tf_op jit(solution)/shard_map/while/body/eval_jaxpr/ppermute | solution.py:10
  362.5 6.5 %collective-permute-start = (f32[4,64,128]{2,1,0:T(8,128)S(1)}, f32[4,64,128]{2,1,0:T(8,128)S(1)}, u32[]{:S(2)}, u32[]{:S(2)}) collective-permute-start(f32[4,64,128]{2,1,0:T(8,128)S(1)} %multiply_add_fusion.2), channel_id=1, source_target_pairs={{16,0},{32,16},{48,32},{64,48},{80,64},{96,80},{112,96},{128,112},... | collective-permute-start | bytes 393224 | tf_op jit(solution)/shard_map/while/body/eval_jaxpr/ppermute | solution.py:10
  409.2 33.6 %all-gather.1 = f32[32,3,4]{2,1,0:T(4,128)S(1)} all-gather(f32[1,3,4]{2,1,0:T(4,128)S(1)} %maximum_bitcast_fusion), channel_id=2, replica_groups=mesh['seq'=32,'head'=16] {'seq'}, dimensions={0}, use_global_device_ids=true | all-gather | bytes 1584 | tf_op jit(solution)/shard_map/all_gather | solution.py:102
  443.4 82.9 %reduce-scatter.3.cloned.1.call-done = bf16[256,256]{0,1:T(8,128)(2,1)} async-done(((bf16[4096,256]{0,1:T(8,128)(2,1)}), bf16[256,256]{0,1:T(8,128)(2,1)}) %reduce-scatter.3.cloned.1.call-update) | async-done | bytes 131088 | tf_op jit(solution)/shard_map/reduce_scatter | solution.py:92
  527.9 109.4 %reduce-scatter.5.cloned.1.call-done = bf16[16,256]{1,0:T(8,128)(2,1)} async-done(((bf16[256,256]{1,0:T(8,128)(2,1)}), bf16[16,256]{1,0:T(8,128)(2,1)}) %reduce-scatter.5.cloned.1.call-update) | async-done | bytes 8208 | tf_op jit(solution)/shard_map/reduce_scatter | solution.py:100
  (140 shorter events, 125.2 us)
Async XLA Ops:
  7.2 110.5 %all-gather.4.cloned.1.call-start = ((), (), s32[]{:S(2)}) async-start(), calls=%async_computation.2 | async-start | bytes 2228224 | tf_op jit(solution)/shard_map/all_gather | solution.py:20
  7.9 518.3 %reduce-scatter.3.cloned.1.call-start = ((), (), s32[]{:S(2)}) async-start(), calls=%async_computation.3 | async-start | bytes 2228224 | tf_op jit(solution)/shard_map/reduce_scatter | solution.py:92
  126.7 9.0 %collective-permute-start = (f32[4,64,128]{2,1,0:T(8,128)S(1)}, f32[4,64,128]{2,1,0:T(8,128)S(1)}, u32[]{:S(2)}, u32[]{:S(2)}) collective-permute-start(f32[4,64,128]{2,1,0:T(8,128)S(1)} %multiply_add_fusion.2), channel_id=1, source_target_pairs={{16,0},{32,16},{48,32},{64,48},{80,64},{96,80},{112,96},{128,112},... | collective-permute-start | bytes 393224 | tf_op jit(solution)/shard_map/while/body/eval_jaxpr/ppermute | solution.py:10
  135.8 9.0 %collective-permute-start = (f32[4,64,128]{2,1,0:T(8,128)S(1)}, f32[4,64,128]{2,1,0:T(8,128)S(1)}, u32[]{:S(2)}, u32[]{:S(2)}) collective-permute-start(f32[4,64,128]{2,1,0:T(8,128)S(1)} %multiply_add_fusion.2), channel_id=1, source_target_pairs={{16,0},{32,16},{48,32},{64,48},{80,64},{96,80},{112,96},{128,112},... | collective-permute-start | bytes 393224 | tf_op jit(solution)/shard_map/while/body/eval_jaxpr/ppermute | solution.py:10
  144.9 9.0 %collective-permute-start = (f32[4,64,128]{2,1,0:T(8,128)S(1)}, f32[4,64,128]{2,1,0:T(8,128)S(1)}, u32[]{:S(2)}, u32[]{:S(2)}) collective-permute-start(f32[4,64,128]{2,1,0:T(8,128)S(1)} %multiply_add_fusion.2), channel_id=1, source_target_pairs={{16,0},{32,16},{48,32},{64,48},{80,64},{96,80},{112,96},{128,112},... | collective-permute-start | bytes 393224 | tf_op jit(solution)/shard_map/while/body/eval_jaxpr/ppermute | solution.py:10
  153.9 9.0 %collective-permute-start = (f32[4,64,128]{2,1,0:T(8,128)S(1)}, f32[4,64,128]{2,1,0:T(8,128)S(1)}, u32[]{:S(2)}, u32[]{:S(2)}) collective-permute-start(f32[4,64,128]{2,1,0:T(8,128)S(1)} %multiply_add_fusion.2), channel_id=1, source_target_pairs={{16,0},{32,16},{48,32},{64,48},{80,64},{96,80},{112,96},{128,112},... | collective-permute-start | bytes 393224 | tf_op jit(solution)/shard_map/while/body/eval_jaxpr/ppermute | solution.py:10
  163.0 9.0 %collective-permute-start = (f32[4,64,128]{2,1,0:T(8,128)S(1)}, f32[4,64,128]{2,1,0:T(8,128)S(1)}, u32[]{:S(2)}, u32[]{:S(2)}) collective-permute-start(f32[4,64,128]{2,1,0:T(8,128)S(1)} %multiply_add_fusion.2), channel_id=1, source_target_pairs={{16,0},{32,16},{48,32},{64,48},{80,64},{96,80},{112,96},{128,112},... | collective-permute-start | bytes 393224 | tf_op jit(solution)/shard_map/while/body/eval_jaxpr/ppermute | solution.py:10
  172.1 9.0 %collective-permute-start = (f32[4,64,128]{2,1,0:T(8,128)S(1)}, f32[4,64,128]{2,1,0:T(8,128)S(1)}, u32[]{:S(2)}, u32[]{:S(2)}) collective-permute-start(f32[4,64,128]{2,1,0:T(8,128)S(1)} %multiply_add_fusion.2), channel_id=1, source_target_pairs={{16,0},{32,16},{48,32},{64,48},{80,64},{96,80},{112,96},{128,112},... | collective-permute-start | bytes 393224 | tf_op jit(solution)/shard_map/while/body/eval_jaxpr/ppermute | solution.py:10
  181.1 9.0 %collective-permute-start = (f32[4,64,128]{2,1,0:T(8,128)S(1)}, f32[4,64,128]{2,1,0:T(8,128)S(1)}, u32[]{:S(2)}, u32[]{:S(2)}) collective-permute-start(f32[4,64,128]{2,1,0:T(8,128)S(1)} %multiply_add_fusion.2), channel_id=1, source_target_pairs={{16,0},{32,16},{48,32},{64,48},{80,64},{96,80},{112,96},{128,112},... | collective-permute-start | bytes 393224 | tf_op jit(solution)/shard_map/while/body/eval_jaxpr/ppermute | solution.py:10
  190.2 9.0 %collective-permute-start = (f32[4,64,128]{2,1,0:T(8,128)S(1)}, f32[4,64,128]{2,1,0:T(8,128)S(1)}, u32[]{:S(2)}, u32[]{:S(2)}) collective-permute-start(f32[4,64,128]{2,1,0:T(8,128)S(1)} %multiply_add_fusion.2), channel_id=1, source_target_pairs={{16,0},{32,16},{48,32},{64,48},{80,64},{96,80},{112,96},{128,112},... | collective-permute-start | bytes 393224 | tf_op jit(solution)/shard_map/while/body/eval_jaxpr/ppermute | solution.py:10
  199.3 9.0 %collective-permute-start = (f32[4,64,128]{2,1,0:T(8,128)S(1)}, f32[4,64,128]{2,1,0:T(8,128)S(1)}, u32[]{:S(2)}, u32[]{:S(2)}) collective-permute-start(f32[4,64,128]{2,1,0:T(8,128)S(1)} %multiply_add_fusion.2), channel_id=1, source_target_pairs={{16,0},{32,16},{48,32},{64,48},{80,64},{96,80},{112,96},{128,112},... | collective-permute-start | bytes 393224 | tf_op jit(solution)/shard_map/while/body/eval_jaxpr/ppermute | solution.py:10
  208.4 9.0 %collective-permute-start = (f32[4,64,128]{2,1,0:T(8,128)S(1)}, f32[4,64,128]{2,1,0:T(8,128)S(1)}, u32[]{:S(2)}, u32[]{:S(2)}) collective-permute-start(f32[4,64,128]{2,1,0:T(8,128)S(1)} %multiply_add_fusion.2), channel_id=1, source_target_pairs={{16,0},{32,16},{48,32},{64,48},{80,64},{96,80},{112,96},{128,112},... | collective-permute-start | bytes 393224 | tf_op jit(solution)/shard_map/while/body/eval_jaxpr/ppermute | solution.py:10
  217.4 9.0 %collective-permute-start = (f32[4,64,128]{2,1,0:T(8,128)S(1)}, f32[4,64,128]{2,1,0:T(8,128)S(1)}, u32[]{:S(2)}, u32[]{:S(2)}) collective-permute-start(f32[4,64,128]{2,1,0:T(8,128)S(1)} %multiply_add_fusion.2), channel_id=1, source_target_pairs={{16,0},{32,16},{48,32},{64,48},{80,64},{96,80},{112,96},{128,112},... | collective-permute-start | bytes 393224 | tf_op jit(solution)/shard_map/while/body/eval_jaxpr/ppermute | solution.py:10
  226.5 9.0 %collective-permute-start = (f32[4,64,128]{2,1,0:T(8,128)S(1)}, f32[4,64,128]{2,1,0:T(8,128)S(1)}, u32[]{:S(2)}, u32[]{:S(2)}) collective-permute-start(f32[4,64,128]{2,1,0:T(8,128)S(1)} %multiply_add_fusion.2), channel_id=1, source_target_pairs={{16,0},{32,16},{48,32},{64,48},{80,64},{96,80},{112,96},{128,112},... | collective-permute-start | bytes 393224 | tf_op jit(solution)/shard_map/while/body/eval_jaxpr/ppermute | solution.py:10
  235.6 9.0 %collective-permute-start = (f32[4,64,128]{2,1,0:T(8,128)S(1)}, f32[4,64,128]{2,1,0:T(8,128)S(1)}, u32[]{:S(2)}, u32[]{:S(2)}) collective-permute-start(f32[4,64,128]{2,1,0:T(8,128)S(1)} %multiply_add_fusion.2), channel_id=1, source_target_pairs={{16,0},{32,16},{48,32},{64,48},{80,64},{96,80},{112,96},{128,112},... | collective-permute-start | bytes 393224 | tf_op jit(solution)/shard_map/while/body/eval_jaxpr/ppermute | solution.py:10
  244.6 9.0 %collective-permute-start = (f32[4,64,128]{2,1,0:T(8,128)S(1)}, f32[4,64,128]{2,1,0:T(8,128)S(1)}, u32[]{:S(2)}, u32[]{:S(2)}) collective-permute-start(f32[4,64,128]{2,1,0:T(8,128)S(1)} %multiply_add_fusion.2), channel_id=1, source_target_pairs={{16,0},{32,16},{48,32},{64,48},{80,64},{96,80},{112,96},{128,112},... | collective-permute-start | bytes 393224 | tf_op jit(solution)/shard_map/while/body/eval_jaxpr/ppermute | solution.py:10
  253.7 9.0 %collective-permute-start = (f32[4,64,128]{2,1,0:T(8,128)S(1)}, f32[4,64,128]{2,1,0:T(8,128)S(1)}, u32[]{:S(2)}, u32[]{:S(2)}) collective-permute-start(f32[4,64,128]{2,1,0:T(8,128)S(1)} %multiply_add_fusion.2), channel_id=1, source_target_pairs={{16,0},{32,16},{48,32},{64,48},{80,64},{96,80},{112,96},{128,112},... | collective-permute-start | bytes 393224 | tf_op jit(solution)/shard_map/while/body/eval_jaxpr/ppermute | solution.py:10
  262.8 9.0 %collective-permute-start = (f32[4,64,128]{2,1,0:T(8,128)S(1)}, f32[4,64,128]{2,1,0:T(8,128)S(1)}, u32[]{:S(2)}, u32[]{:S(2)}) collective-permute-start(f32[4,64,128]{2,1,0:T(8,128)S(1)} %multiply_add_fusion.2), channel_id=1, source_target_pairs={{16,0},{32,16},{48,32},{64,48},{80,64},{96,80},{112,96},{128,112},... | collective-permute-start | bytes 393224 | tf_op jit(solution)/shard_map/while/body/eval_jaxpr/ppermute | solution.py:10
  271.8 9.0 %collective-permute-start = (f32[4,64,128]{2,1,0:T(8,128)S(1)}, f32[4,64,128]{2,1,0:T(8,128)S(1)}, u32[]{:S(2)}, u32[]{:S(2)}) collective-permute-start(f32[4,64,128]{2,1,0:T(8,128)S(1)} %multiply_add_fusion.2), channel_id=1, source_target_pairs={{16,0},{32,16},{48,32},{64,48},{80,64},{96,80},{112,96},{128,112},... | collective-permute-start | bytes 393224 | tf_op jit(solution)/shard_map/while/body/eval_jaxpr/ppermute | solution.py:10
  280.9 9.0 %collective-permute-start = (f32[4,64,128]{2,1,0:T(8,128)S(1)}, f32[4,64,128]{2,1,0:T(8,128)S(1)}, u32[]{:S(2)}, u32[]{:S(2)}) collective-permute-start(f32[4,64,128]{2,1,0:T(8,128)S(1)} %multiply_add_fusion.2), channel_id=1, source_target_pairs={{16,0},{32,16},{48,32},{64,48},{80,64},{96,80},{112,96},{128,112},... | collective-permute-start | bytes 393224 | tf_op jit(solution)/shard_map/while/body/eval_jaxpr/ppermute | solution.py:10
  290.0 9.0 %collective-permute-start = (f32[4,64,128]{2,1,0:T(8,128)S(1)}, f32[4,64,128]{2,1,0:T(8,128)S(1)}, u32[]{:S(2)}, u32[]{:S(2)}) collective-permute-start(f32[4,64,128]{2,1,0:T(8,128)S(1)} %multiply_add_fusion.2), channel_id=1, source_target_pairs={{16,0},{32,16},{48,32},{64,48},{80,64},{96,80},{112,96},{128,112},... | collective-permute-start | bytes 393224 | tf_op jit(solution)/shard_map/while/body/eval_jaxpr/ppermute | solution.py:10
  299.0 9.0 %collective-permute-start = (f32[4,64,128]{2,1,0:T(8,128)S(1)}, f32[4,64,128]{2,1,0:T(8,128)S(1)}, u32[]{:S(2)}, u32[]{:S(2)}) collective-permute-start(f32[4,64,128]{2,1,0:T(8,128)S(1)} %multiply_add_fusion.2), channel_id=1, source_target_pairs={{16,0},{32,16},{48,32},{64,48},{80,64},{96,80},{112,96},{128,112},... | collective-permute-start | bytes 393224 | tf_op jit(solution)/shard_map/while/body/eval_jaxpr/ppermute | solution.py:10
  308.1 9.0 %collective-permute-start = (f32[4,64,128]{2,1,0:T(8,128)S(1)}, f32[4,64,128]{2,1,0:T(8,128)S(1)}, u32[]{:S(2)}, u32[]{:S(2)}) collective-permute-start(f32[4,64,128]{2,1,0:T(8,128)S(1)} %multiply_add_fusion.2), channel_id=1, source_target_pairs={{16,0},{32,16},{48,32},{64,48},{80,64},{96,80},{112,96},{128,112},... | collective-permute-start | bytes 393224 | tf_op jit(solution)/shard_map/while/body/eval_jaxpr/ppermute | solution.py:10
  317.2 9.0 %collective-permute-start = (f32[4,64,128]{2,1,0:T(8,128)S(1)}, f32[4,64,128]{2,1,0:T(8,128)S(1)}, u32[]{:S(2)}, u32[]{:S(2)}) collective-permute-start(f32[4,64,128]{2,1,0:T(8,128)S(1)} %multiply_add_fusion.2), channel_id=1, source_target_pairs={{16,0},{32,16},{48,32},{64,48},{80,64},{96,80},{112,96},{128,112},... | collective-permute-start | bytes 393224 | tf_op jit(solution)/shard_map/while/body/eval_jaxpr/ppermute | solution.py:10
  326.2 9.0 %collective-permute-start = (f32[4,64,128]{2,1,0:T(8,128)S(1)}, f32[4,64,128]{2,1,0:T(8,128)S(1)}, u32[]{:S(2)}, u32[]{:S(2)}) collective-permute-start(f32[4,64,128]{2,1,0:T(8,128)S(1)} %multiply_add_fusion.2), channel_id=1, source_target_pairs={{16,0},{32,16},{48,32},{64,48},{80,64},{96,80},{112,96},{128,112},... | collective-permute-start | bytes 393224 | tf_op jit(solution)/shard_map/while/body/eval_jaxpr/ppermute | solution.py:10
  335.3 9.0 %collective-permute-start = (f32[4,64,128]{2,1,0:T(8,128)S(1)}, f32[4,64,128]{2,1,0:T(8,128)S(1)}, u32[]{:S(2)}, u32[]{:S(2)}) collective-permute-start(f32[4,64,128]{2,1,0:T(8,128)S(1)} %multiply_add_fusion.2), channel_id=1, source_target_pairs={{16,0},{32,16},{48,32},{64,48},{80,64},{96,80},{112,96},{128,112},... | collective-permute-start | bytes 393224 | tf_op jit(solution)/shard_map/while/body/eval_jaxpr/ppermute | solution.py:10
  344.4 9.0 %collective-permute-start = (f32[4,64,128]{2,1,0:T(8,128)S(1)}, f32[4,64,128]{2,1,0:T(8,128)S(1)}, u32[]{:S(2)}, u32[]{:S(2)}) collective-permute-start(f32[4,64,128]{2,1,0:T(8,128)S(1)} %multiply_add_fusion.2), channel_id=1, source_target_pairs={{16,0},{32,16},{48,32},{64,48},{80,64},{96,80},{112,96},{128,112},... | collective-permute-start | bytes 393224 | tf_op jit(solution)/shard_map/while/body/eval_jaxpr/ppermute | solution.py:10
  353.4 9.0 %collective-permute-start = (f32[4,64,128]{2,1,0:T(8,128)S(1)}, f32[4,64,128]{2,1,0:T(8,128)S(1)}, u32[]{:S(2)}, u32[]{:S(2)}) collective-permute-start(f32[4,64,128]{2,1,0:T(8,128)S(1)} %multiply_add_fusion.2), channel_id=1, source_target_pairs={{16,0},{32,16},{48,32},{64,48},{80,64},{96,80},{112,96},{128,112},... | collective-permute-start | bytes 393224 | tf_op jit(solution)/shard_map/while/body/eval_jaxpr/ppermute | solution.py:10
  362.5 9.0 %collective-permute-start = (f32[4,64,128]{2,1,0:T(8,128)S(1)}, f32[4,64,128]{2,1,0:T(8,128)S(1)}, u32[]{:S(2)}, u32[]{:S(2)}) collective-permute-start(f32[4,64,128]{2,1,0:T(8,128)S(1)} %multiply_add_fusion.2), channel_id=1, source_target_pairs={{16,0},{32,16},{48,32},{64,48},{80,64},{96,80},{112,96},{128,112},... | collective-permute-start | bytes 393224 | tf_op jit(solution)/shard_map/while/body/eval_jaxpr/ppermute | solution.py:10
  380.6 9.0 %collective-permute-start = (f32[4,64,128]{2,1,0:T(8,128)S(1)}, f32[4,64,128]{2,1,0:T(8,128)S(1)}, u32[]{:S(2)}, u32[]{:S(2)}) collective-permute-start(f32[4,64,128]{2,1,0:T(8,128)S(1)} %multiply_add_fusion.2), channel_id=1, source_target_pairs={{16,0},{32,16},{48,32},{64,48},{80,64},{96,80},{112,96},{128,112},... | collective-permute-start | bytes 393224 | tf_op jit(solution)/shard_map/while/body/eval_jaxpr/ppermute | solution.py:10
  389.7 9.0 %collective-permute-start = (f32[4,64,128]{2,1,0:T(8,128)S(1)}, f32[4,64,128]{2,1,0:T(8,128)S(1)}, u32[]{:S(2)}, u32[]{:S(2)}) collective-permute-start(f32[4,64,128]{2,1,0:T(8,128)S(1)} %multiply_add_fusion.2), channel_id=1, source_target_pairs={{16,0},{32,16},{48,32},{64,48},{80,64},{96,80},{112,96},{128,112},... | collective-permute-start | bytes 393224 | tf_op jit(solution)/shard_map/while/body/eval_jaxpr/ppermute | solution.py:10
  402.1 235.2 %reduce-scatter.5.cloned.1.call-start = ((), (), s32[]{:S(2)}) async-start(), calls=%async_computation.4 | async-start | bytes 139264 | tf_op jit(solution)/shard_map/reduce_scatter | solution.py:100
  (9 other events, 969.1 us)
Sparse Core Ops, SparseCore 0:
  11.0 106.6 all-gather.3
  402.2 123.9 reduce-scatter.2
  531.4 105.8 reduce-scatter.4
